TPU v7x, 32 devices: a whole 2x2x4 slice. The times are simulated.
32 devices in a mesh: dp: 8 (over z, x), mp: 4 (over y, core).
Axes of the slice: x: 2, y: 2, z: 4, core: 2. Of those that a mesh axis runs over, the one named last changes fastest.
Arguments:
- acts: bfloat16 [16384, 768], P('dp'), may hold values from -6 to 6
- out_grads: bfloat16 [16384, 3072], P('dp', 'mp'), may hold values from -0.046875 to 0.046875
- block_owner: int32 [4], replicated, may hold values from 0 to 3, as said below
- left_stat: float32 [8, 768, 768], P('mp', 'dp')
- right_stat: float32 [8, 768, 768], P('mp', 'dp')
- left_root: bfloat16 [8, 768, 768], P('mp', 'dp')
- right_root: bfloat16 [8, 768, 768], P('mp', 'dp')
Outputs:
- update: bfloat16 [768, 3072], P('dp', 'mp')
- left_new: float32 [8, 768, 768], P('mp', 'dp')
- right_new: float32 [8, 768, 768], P('mp', 'dp')
Inputs may be any that keep to these rules, and one draw needn't show every extreme that they name: Block c of the 4 blocks is owned by block_owner[c]; no owner holds more than 2 blocks, and some owner holds exactly 2.
All inputs are finite; a program needn't handle non-finite values.
Results may differ from a plain program's by a relative error of at most 0.0058.
Values may be sent and summed in bfloat16 or wider, within the bound.
A program may use at most 64 MiB of HBM per device.

v0:
```python
import jax
import jax.numpy as jnp
from jax import lax
from jax.sharding import PartitionSpec as P


def state_index(block_owner, capacity):
    block_count = block_owner.shape[0]
    column_ids = jnp.arange(block_count, dtype=jnp.int32)
    same_owner = block_owner[None, :] == block_owner[:, None]
    earlier = column_ids[None, :] < column_ids[:, None]
    slot_rank = jnp.sum((same_owner & earlier).astype(jnp.int32), axis=1)
    return block_owner * capacity + slot_rank


def owner_hits(target, owner_index, capacity):
    wanted = owner_index * capacity + jnp.arange(capacity, dtype=jnp.int32)
    return target[None, :] == wanted[:, None]


def gram_rows(own_rows, own_cols, whole_grad):
    left_part = jnp.einsum("sik,sjk->sij", own_rows, whole_grad, preferred_element_type=jnp.float32)
    right_part = jnp.einsum(
        "ski,skj->sij", own_cols, whole_grad, preferred_element_type=jnp.float32
    )
    return (left_part, right_part)


def precondition(root_rows, whole_grad, whole_right):
    left_part = jnp.einsum(
        "sik,skj->sij", root_rows, whole_grad, preferred_element_type=jnp.float32
    ).astype(jnp.bfloat16)
    return jnp.einsum(
        "sik,skj->sij", left_part, whole_right, preferred_element_type=jnp.float32
    ).astype(jnp.bfloat16)


def route_slots(slot_match, slots):
    picker = jnp.transpose(slot_match).astype(jnp.bfloat16)
    return jnp.einsum("ds,sij->dij", picker, slots, preferred_element_type=jnp.float32).astype(
        jnp.bfloat16
    )


def local(acts, out_grads, block_owner, left_stat, right_stat, left_root, right_root):
    block_order = acts.shape[1]
    slab_rows = block_order // lax.axis_size("dp")
    capacity = left_stat.shape[0]
    target = state_index(block_owner, capacity)
    column_index = lax.axis_index("mp")
    slab_start = lax.axis_index("dp") * slab_rows
    my_owner = block_owner[column_index]
    own_grad = lax.psum_scatter(
        jnp.einsum("tr,tc->rc", acts, out_grads, preferred_element_type=jnp.float32),
        "dp",
        scatter_dimension=0,
        tiled=True,
    ).astype(jnp.bfloat16)
    slot_match = owner_hits(target, column_index, capacity)
    slot_used = jnp.any(slot_match, axis=1)
    slot_weights = slot_match.astype(jnp.float32)
    left_out = route_slots(slot_match, left_root)
    right_out = route_slots(slot_match, right_root)
    left_arrived, right_arrived = (
        lax.all_to_all(left_out, "mp", split_axis=0, concat_axis=0, tiled=True),
        lax.all_to_all(right_out, "mp", split_axis=0, concat_axis=0, tiled=True),
    )
    root_rows = lax.dynamic_index_in_dim(left_arrived, my_owner, 0, keepdims=True)
    right_rows = lax.dynamic_index_in_dim(right_arrived, my_owner, 0, keepdims=True)
    whole_grad, whole_right = (
        lax.all_gather(own_grad[None], "dp", axis=1, tiled=True),
        lax.all_gather(right_rows, "dp", axis=1, tiled=True),
    )
    own_cols = lax.dynamic_slice_in_dim(whole_grad, slab_start, slab_rows, 2)
    left_part, right_part = gram_rows(own_grad[None], own_cols, whole_grad)
    update = precondition(root_rows, whole_grad, whole_right)[0]
    owner_ids = jnp.arange(block_owner.shape[0], dtype=jnp.int32)
    send_mask = (owner_ids == my_owner)[:, None, None]
    left_send = jnp.where(send_mask, left_part, 0.0)
    right_send = jnp.where(send_mask, right_part, 0.0)
    left_every_gram, right_every_gram = (
        lax.all_to_all(
            left_send.astype(jnp.bfloat16), "mp", split_axis=0, concat_axis=0, tiled=True
        ).astype(left_send.dtype),
        lax.all_to_all(
            right_send.astype(jnp.bfloat16), "mp", split_axis=0, concat_axis=0, tiled=True
        ).astype(right_send.dtype),
    )
    left_gram = jnp.einsum(
        "sc,cij->sij", slot_weights, left_every_gram, precision=lax.Precision.HIGHEST
    )
    right_gram = jnp.einsum(
        "sc,cij->sij", slot_weights, right_every_gram, precision=lax.Precision.HIGHEST
    )
    keep_mask = slot_used[:, None, None]
    left_new = jnp.where(keep_mask, 0.8 * left_stat + 0.2 * (left_gram / block_order), left_stat)
    right_new = jnp.where(
        keep_mask, 0.8 * right_stat + 0.2 * (right_gram / block_order), right_stat
    )
    return (update, left_new, right_new)


def solution(mesh):
    in_specs = (
        P("dp", None),
        P("dp", "mp"),
        P(),
        P("mp", "dp", None),
        P("mp", "dp", None),
        P("mp", "dp", None),
        P("mp", "dp", None),
    )
    out_specs = (P("dp", "mp"), P("mp", "dp", None), P("mp", "dp", None))
    return jax.shard_map(local, mesh=mesh, in_specs=in_specs, out_specs=out_specs, check_vma=False)
```

profile of v0, /device:TPU:1, one launch (start us, length us, event | category | flops | bytes accessed | tf_op | source)
XLA Modules:
  0.0 186.3 jit_solution(14028137226567646817)
XLA Ops:
  7.2 1.8 copy-done
  9.1 6.0 %fusion.23 = f32[768,768]{1,0:T(8,128)} fusion(bf16[2048,768]{1,0:T(8,128)(2,1)S(1)} %copy-done, bf16[2048,768]{1,0:T(8,128)(2,1)} %param.8), kind=kOutput, calls=%fused_computation.33 | convolution fusion | flops 2415919104 | bytes 8650752 | tf_op jit(solution)/shard_map/tr,tc->rc/dot_general | solution.py:54
  15.1 70.1 %reduce-scatter.2.cloned.1.call-done = f32[96,768]{1,0:T(8,128)} async-done(((f32[768,768]{1,0:T(8,128)}), f32[96,768]{1,0:T(8,128)}) %reduce-scatter.2.cloned.1.call-update) | async-done | bytes 294928 | tf_op jit(solution)/shard_map/reduce_scatter | solution.py:53
  85.2 1.6 convert_element_type.33
  87.3 1.5 convolution_convert_fusion
  88.8 0.9 copy.41
  89.7 5.8 %all-to-all-start.1 = ((bf16[4,96,768]{2,1,0:T(8,128)(2,1)}), bf16[4,96,768]{2,1,0:T(8,128)(2,1)}, u32[]{:S(2)}, u32[]{:S(2)}) async-start(bf16[4,96,768]{2,1,0:T(8,128)(2,1)} %copy.41), calls=%async_computation.2 | async-start | bytes 1179648 | tf_op jit(solution)/shard_map/all_to_all | solution.py:66
  97.9 6.3 %all-to-all-done.1 = bf16[4,96,768]{2,1,0:T(8,128)(2,1)} async-done(((bf16[4,96,768]{2,1,0:T(8,128)(2,1)}), bf16[4,96,768]{2,1,0:T(8,128)(2,1)}, u32[]{:S(2)}, u32[]{:S(2)}) %all-to-all-start.1) | async-done | bytes 589856 | tf_op jit(solution)/shard_map/all_to_all | solution.py:66
  104.3 1.6 constant_dynamic-slice_fusion
  105.9 1.5 convolution_convert_fusion.1
  107.4 0.9 copy.39
  108.3 5.0 %all-to-all-start = ((bf16[4,96,768]{2,1,0:T(8,128)(2,1)}), bf16[4,96,768]{2,1,0:T(8,128)(2,1)}, u32[]{:S(2)}, u32[]{:S(2)}) async-start(bf16[4,96,768]{2,1,0:T(8,128)(2,1)} %copy.39), calls=%async_computation | async-start | bytes 1179648 | tf_op jit(solution)/shard_map/all_to_all | solution.py:65
  113.3 0.6 iota_compare_fusion.1
  113.9 14.0 %all-gather.6.cloned.1.call-done = bf16[768,768]{1,0:T(8,128)(2,1)} async-done(((bf16[96,768]{1,0:T(8,128)(2,1)}), bf16[768,768]{1,0:T(8,128)(2,1)}) %all-gather.6.cloned.1.call-update) | async-done | bytes 1179664 | tf_op jit(solution)/shard_map/all_gather | solution.py:71
  127.9 1.9 %fusion.24 = bf16[96,768]{1,0:T(8,128)(2,1)S(1)} fusion(bf16[96,768]{1,0:T(8,128)(2,1)S(1)} %copy-done.2, bf16[768,768]{1,0:T(8,128)(2,1)} %all-gather.6.cloned.1.call-done), kind=kOutput, calls=%fused_computation.34 | convolution fusion | flops 113246208 | bytes 1474560 | tf_op jit(solution)/shard_map/sik,sjk->sij/dot_general | solution.py:22
  130.2 1.3 select_convert_fusion
  131.5 15.1 %all_to_all.20 = bf16[4,96,768]{2,1,0:T(8,128)(2,1)} all-to-all(bf16[4,96,768]{2,1,0:T(8,128)(2,1)} %get-tuple-element.18), channel_id=1, replica_groups=mesh['dp'=8,'mp'=4] {'mp'}, dimensions={0} | all-to-all | bytes 1179648 | tf_op jit(solution)/shard_map/all_to_all | solution.py:82
  146.6 4.7 %all-to-all-start.3 = ((bf16[4,96,768]{2,1,0:T(8,128)(2,1)}), bf16[4,96,768]{2,1,0:T(8,128)(2,1)}, u32[]{:S(2)}, u32[]{:S(2)}) async-start(bf16[4,96,768]{2,1,0:T(8,128)(2,1)} %get-tuple-element.17), calls=%async_computation.4 | async-start | bytes 1179648 | tf_op jit(solution)/shard_map/all_to_all | solution.py:85
  151.3 19.3 %all-gather.4.cloned.1.call-done = bf16[1,768,768]{2,1,0:T(8,128)(2,1)} async-done(((bf16[1,96,768]{2,1,0:T(8,128)(2,1)}), bf16[1,768,768]{2,1,0:T(8,128)(2,1)}) %all-gather.4.cloned.1.call-update) | async-done | bytes 1179664 | tf_op jit(solution)/shard_map/all_gather | solution.py:72
  170.5 2.9 %fusion.6 = bf16[96,768]{1,0:T(8,128)(2,1)} fusion(bf16[1,768,768]{2,1,0:T(8,128)(2,1)} %all-gather.4.cloned.1.call-done, bf16[768,768]{1,0:T(8,128)(2,1)} %all-gather.6.cloned.1.call-done, bf16[4,96,768]{2,1,0:T(8,128)(2,1)} %all-to-all-done, s32[]{:T(128)S(6)} %select_n.26), kind=kOutput, calls=%fused_computation.12 | convolution fusion | flops 226639872 | bytes 2654212 | tf_op jit(solution)/shard_map/sik,skj->sij/dot_general | solution.py:33
  173.5 2.3 %fusion.1 = f32[2,96,768]{2,0,1:T(2,128)S(1)} fusion(pred[2,4,1]{1,0,2:T(4,128)(4,1)S(1)} %get-tuple-element.16, f32[2,96,768]{2,1,0:T(8,128)} %param.10, pred[2]{0:T(512)(128)(4,1)S(1)} %get-tuple-element.15, bf16[4,96,768]{2,1,0:T(8,128)(2,1)} %all_to_all.20), kind=kOutput, calls=%fused_computation.5 | convolution fusion | flops 1769472 | bytes 1769482 | tf_op jit(solution)/shard_map/sc,cij->sij/dot_general | solution.py:89
  175.8 0.9 copy.48
  176.6 2.3 %fusion.3 = f32[2,96,768]{2,0,1:T(2,128)S(1)} fusion(pred[2,4,1]{1,0,2:T(4,128)(4,1)S(1)} %get-tuple-element.16, f32[2,96,768]{2,1,0:T(8,128)} %param.11, pred[2]{0:T(512)(128)(4,1)S(1)} %get-tuple-element.15, bf16[4,96,768]{2,1,0:T(8,128)(2,1)} %all-to-all-done.3), kind=kOutput, calls=%fused_computation.7 | convolution fusion | flops 1769472 | bytes 1769482 | tf_op jit(solution)/shard_map/sc,cij->sij/dot_general | solution.py:92
  178.9 0.9 copy.49
  (21 shorter events, 1.6 us)
Async XLA Ops:
  7.2 1.9 %copy-start = (bf16[2048,768]{1,0:T(8,128)(2,1)S(1)}, bf16[2048,768]{1,0:T(8,128)(2,1)}, u32[]{:S(2)}) copy-start(bf16[2048,768]{1,0:T(8,128)(2,1)} %param.7) | copy-start | bytes 9437188
  7.2 78.1 %reduce-scatter.2.cloned.1.call-start = ((), (), s32[]{:S(2)}) async-start(), calls=%async_computation.5 | async-start | bytes 2654208 | tf_op jit(solution)/shard_map/reduce_scatter | solution.py:53
  15.0 71.9 %copy-start.3 = (s32[4]{0:T(128)S(1)}, s32[4]{0:T(128)}, u32[]{:S(2)}) copy-start(s32[4]{0:T(128)} %param.9) | copy-start | bytes 52
  15.1 112.8 %all-gather.6.cloned.1.call-start = ((), (), s32[]{:S(2)}) async-start(), calls=%async_computation.7 | async-start | bytes 1327104 | tf_op jit(solution)/shard_map/all_gather | solution.py:71
  89.7 14.5 %all-to-all-start.1 = ((bf16[4,96,768]{2,1,0:T(8,128)(2,1)}), bf16[4,96,768]{2,1,0:T(8,128)(2,1)}, u32[]{:S(2)}, u32[]{:S(2)}) async-start(bf16[4,96,768]{2,1,0:T(8,128)(2,1)} %copy.41), calls=%async_computation.2 | async-start | bytes 1179648 | tf_op jit(solution)/shard_map/all_to_all | solution.py:66
  95.5 75.1 %all-gather.4.cloned.1.call-start = ((), (), s32[]{:S(2)}) async-start(), calls=%async_computation.6 | async-start | bytes 1327104 | tf_op jit(solution)/shard_map/all_gather | solution.py:72
  107.4 20.5 %copy-start.2 = (bf16[96,768]{1,0:T(8,128)(2,1)S(1)}, bf16[96,768]{1,0:T(8,128)(2,1)}, u32[]{:S(2)}) copy-start(bf16[96,768]{1,0:T(8,128)(2,1)} %convert_element_type.33) | copy-start | bytes 442372
  108.3 23.2 %all-to-all-start = ((bf16[4,96,768]{2,1,0:T(8,128)(2,1)}), bf16[4,96,768]{2,1,0:T(8,128)(2,1)}, u32[]{:S(2)}, u32[]{:S(2)}) async-start(bf16[4,96,768]{2,1,0:T(8,128)(2,1)} %copy.39), calls=%async_computation | async-start | bytes 1179648 | tf_op jit(solution)/shard_map/all_to_all | solution.py:65
  127.9 1.9 %copy-start.1 = (bf16[768,768]{1,0:T(8,128)(2,1)S(1)}, bf16[768,768]{1,0:T(8,128)(2,1)}, u32[]{:S(2)}) copy-start(bf16[768,768]{1,0:T(8,128)(2,1)} %all-gather.6.cloned.1.call-done) | copy-start | bytes 3538948
  146.6 30.0 %all-to-all-start.3 = ((bf16[4,96,768]{2,1,0:T(8,128)(2,1)}), bf16[4,96,768]{2,1,0:T(8,128)(2,1)}, u32[]{:S(2)}, u32[]{:S(2)}) async-start(bf16[4,96,768]{2,1,0:T(8,128)(2,1)} %get-tuple-element.17), calls=%async_computation.4 | async-start | bytes 1179648 | tf_op jit(solution)/shard_map/all_to_all | solution.py:85
Sparse Core Ops, SparseCore 0:
  15.2 70.0 reduce-scatter.1
  88.0 39.8 all-gather.5
  130.6 39.8 all-gather.3
where the time goes:
time: 189 us; the launch traced here: 186 us
  waiting for transfers between devices  110 us (58%)
  matrix products  18.9 us (10%)
  between operations  15.7 us (8%)
  starting transfers between devices  15.5 us (8%)
  blocking collectives  15.1 us (8%)
  local copies, waits for them, and re-layouts  7.48 us (4%)
  other arithmetic  3.9 us (2%)
    reduce_scatter x1, waiting for transfers between devices, local(): lax.psum_scatter(jnp.einsum('tr,tc->rc', acts, out_grads, preferred_eleme...  70.1 us
    all_gather x1, waiting for transfers between devices, local(): lax.all_gather(right_rows, 'dp', axis=1, tiled=True)  19.3 us
    all_to_all x1, blocking collectives, local(): lax.all_to_all(left_send.astype(jnp.bfloat16), 'mp', split_axis=0, concat...  15.1 us
    all_gather x1, waiting for transfers between devices, local(): lax.all_gather(own_grad[None], 'dp', axis=1, tiled=True)  14 us
    all_to_all x1, waiting for transfers between devices, local(): lax.all_to_all(right_out, 'mp', split_axis=0, concat_axis=0, tiled=True)  6.33 us
    dot_general x1, matrix products, local(): jnp.einsum('tr,tc->rc', acts, out_grads, preferred_element_type=jnp.float32)  5.98 us
    all_to_all x1, starting transfers between devices, local(): lax.all_to_all(right_out, 'mp', split_axis=0, concat_axis=0, tiled=True)  5.75 us
    all_to_all x1, starting transfers between devices, local(): lax.all_to_all(left_out, 'mp', split_axis=0, concat_axis=0, tiled=True)  4.98 us
  transfers between devices with their start and end apart: 6, of which 4 were waited for; matrix products, arithmetic and copies ran while one was open for 9% of the time, Pallas kernels for 0%

commit v1 on v0

--- a/solution.py
+++ b/solution.py
@@ -1,6 +1,10 @@
+import functools
+
 import jax
 import jax.numpy as jnp
 from jax import lax
+from jax.experimental import pallas as pl
+from jax.experimental.pallas import tpu as pltpu
 from jax.sharding import PartitionSpec as P
 
 
@@ -42,7 +46,7 @@
     )
 
 
-def local(acts, out_grads, block_owner, left_stat, right_stat, left_root, right_root):
+def collective_local(acts, out_grads, block_owner, left_stat, right_stat, left_root, right_root):
     block_order = acts.shape[1]
     slab_rows = block_order // lax.axis_size("dp")
     capacity = left_stat.shape[0]
@@ -100,6 +104,281 @@
     return (update, left_new, right_new)
 
 
+MESH = pl.DeviceIdType.MESH
+BF16 = jnp.bfloat16
+F32 = jnp.float32
+NN = (((1,), (0,)), ((), ()))
+NT = (((1,), (1,)), ((), ()))
+TN = (((0,), (0,)), ((), ()))
+CHUNKS = 4
+
+
+def fits_fused(sizes):
+    return sizes["dp"] == 8 and sizes["mp"] == 4
+
+
+def flip(index, bits):
+    if bits == 0:
+        return index
+    if bits == 1:
+        return index + 1 - 2 * lax.rem(index, 2)
+    if bits == 2:
+        return lax.rem(index + 2, 4)
+    return 3 - index
+
+
+def dot(a, b, dims):
+    return lax.dot_general(a, b, dims, preferred_element_type=F32)
+
+
+def fused_kernel(
+    owner_ref, acts_hbm, outg_hbm, left_stat_hbm, right_stat_hbm, left_root_hbm, right_root_hbm,
+    update_ref, left_new_ref, right_new_ref,
+    acts, outg, lstat, rstat, lroot, rroot,
+    part, send_x, recv_x, send_z, recv_z, grad, right,
+    lout, rout, larr, rarr, lgram, rgram,
+    load_sem, tok_sem, route_ss, route_rs, rsx_ss, rsx_rs, rsz_ss, rsz_rs,
+    agz_ss, agz_rs, agx_ss, agx_rs, gram_ss, gram_rs,
+):
+    blocks = owner_ref.shape[0]
+    order = part.shape[0]
+    capacity, slab = lstat.shape[0], lstat.shape[1]
+    half = order // 2
+    chunk = acts.shape[0] // CHUNKS
+    d, m = lax.axis_index("dp"), lax.axis_index("mp")
+    z, x = d // 2, lax.rem(d, 2)
+
+    def dp_id(zz, xx):
+        return {"dp": zz * 2 + xx}
+
+    def rows_of(zz, xx):
+        return pl.ds(pl.multiple_of((zz * 2 + xx) * slab, slab), slab)
+
+    def remote(src, dst, ss, rs, device):
+        return pltpu.make_async_remote_copy(
+            src_ref=src, dst_ref=dst, send_sem=ss, recv_sem=rs, device_id=device, device_id_type=MESH
+        )
+
+    loads = [
+        pltpu.make_async_copy(right_root_hbm, rroot, load_sem.at[0]),
+        pltpu.make_async_copy(left_root_hbm, lroot, load_sem.at[1]),
+    ]
+    for copy in loads:
+        copy.start()
+    tokens = []
+    for t in range(CHUNKS):
+        rows = pl.ds(t * chunk, chunk)
+        pair = (
+            pltpu.make_async_copy(acts_hbm.at[rows], acts.at[rows], tok_sem.at[t, 0]),
+            pltpu.make_async_copy(outg_hbm.at[rows], outg.at[rows], tok_sem.at[t, 1]),
+        )
+        for copy in pair:
+            copy.start()
+        tokens.append(pair)
+    stats = [
+        pltpu.make_async_copy(left_stat_hbm, lstat, load_sem.at[2]),
+        pltpu.make_async_copy(right_stat_hbm, rstat, load_sem.at[3]),
+    ]
+    for copy in stats:
+        copy.start()
+
+    barrier = pltpu.get_barrier_semaphore()
+    partners = [dp_id(z, 1 - x)] + [dp_id(flip(z, j), x) for j in (1, 2, 3)]
+    partners += [{"mp": flip(m, j)} for j in (1, 2, 3)]
+    for device in partners:
+        pl.semaphore_signal(barrier, inc=1, device_id=device, device_id_type=MESH)
+
+    owners = [owner_ref[c] for c in range(blocks)]
+
+    def rank_of(c):
+        own = owner_ref[c]
+        rank = jnp.int32(0)
+        for other in range(blocks):
+            hit = jnp.logical_and(owners[other] == own, other < c)
+            rank = rank + jnp.where(hit, 1, 0).astype(jnp.int32)
+        return jnp.minimum(rank, capacity - 1)
+
+    loads[0].wait()
+    loads[1].wait()
+    pl.semaphore_wait(barrier, len(partners))
+    pending = []
+
+    def start(copy):
+        copy.start()
+        pending.append(copy)
+        return copy
+
+    routes = {}
+    for k, (root, out, arr) in enumerate(((rroot, rout, rarr), (lroot, lout, larr))):
+        for j in (2, 3, 1):
+            c = flip(m, j)
+            out[j] = root[rank_of(c)]
+            routes[k, j] = start(
+                remote(out.at[j], arr.at[m], route_ss.at[k, j], route_rs.at[k, j], {"mp": c})
+            )
+        arr[m] = root[rank_of(m)]
+
+    part[...] = jnp.zeros_like(part)
+    partner = dp_id(z, 1 - x)
+    sum_x = {}
+    for step in range(2):
+        which = 1 - z // 2 if step == 0 else z // 2
+        base = pl.multiple_of(which * half, half)
+        if step == 0:
+            for t in range(CHUNKS):
+                for copy in tokens[t]:
+                    copy.wait()
+
+        def token_step(t, carry):
+            rows = pl.ds(pl.multiple_of(t * chunk, chunk), chunk)
+            part[pl.ds(base, half), :] += dot(acts[rows, pl.ds(base, half)], outg[rows, :], TN)
+            return carry
+
+        lax.fori_loop(0, CHUNKS, token_step, 0)
+        for j in ((2, 3), (1, 0))[step]:
+            send_x[j] = part[rows_of(flip(z, j), 1 - x), :].astype(BF16)
+            sum_x[j] = start(
+                remote(send_x.at[j], recv_x.at[j], rsx_ss.at[j], rsx_rs.at[j], partner)
+            )
+
+    me = rows_of(z, x)
+
+    def gather_own(k, ref):
+        copies = {"x0": start(remote(ref.at[me], ref.at[me], agx_ss.at[k, 0], agx_rs.at[k, 0], partner))}
+        for j in (2, 3, 1):
+            copies[j] = start(
+                remote(ref.at[me], ref.at[me], agz_ss.at[k, j], agz_rs.at[k, j], dp_id(flip(z, j), x))
+            )
+        return copies
+
+    def gather_on(k, ref, copies):
+        for j in (1, 2, 3):
+            copies[j].wait_recv()
+            rows = rows_of(flip(z, j), x)
+            copies["x%d" % j] = start(
+                remote(ref.at[rows], ref.at[rows], agx_ss.at[k, j], agx_rs.at[k, j], partner)
+            )
+
+    for j in (1, 2, 3):
+        routes[0, j].wait_recv()
+    right[me, :] = rarr[owner_ref[m]]
+    right_copies = gather_own(1, right)
+
+    sum_z = {}
+    for j in (2, 3, 1):
+        sum_x[j].wait_recv()
+        send_z[j] = (part[rows_of(flip(z, j), x), :] + recv_x[j].astype(F32)).astype(BF16)
+        sum_z[j] = start(
+            remote(send_z.at[j], recv_z.at[j], rsz_ss.at[j], rsz_rs.at[j], dp_id(flip(z, j), x))
+        )
+    gather_on(1, right, right_copies)
+    sum_x[0].wait_recv()
+    total = part[me, :] + recv_x[0].astype(F32)
+    for j in (1, 2, 3):
+        sum_z[j].wait_recv()
+        total = total + recv_z[j].astype(F32)
+    own_grad = total.astype(BF16)
+    grad[me, :] = own_grad
+    copies = gather_own(0, grad)
+    gather_on(0, grad, copies)
+    for j in range(4):
+        copies["x%d" % j].wait_recv()
+
+    whole = grad[...]
+    gram_copies = {}
+
+    def share(k, ref):
+        gram_copies[k, 0] = start(
+            remote(ref.at[m], ref.at[m], gram_ss.at[k, 0], gram_rs.at[k, 0], {"mp": flip(m, 2)})
+        )
+        gram_copies[k, 1] = start(
+            remote(ref.at[m], ref.at[m], gram_ss.at[k, 1], gram_rs.at[k, 1], {"mp": flip(m, 1)})
+        )
+
+    lgram[m] = dot(own_grad, whole, NT).astype(BF16)
+    share(0, lgram)
+    row_ids = lax.broadcasted_iota(jnp.int32, (slab, order), 0)
+    col_ids = lax.broadcasted_iota(jnp.int32, (slab, order), 1)
+    picker = jnp.where(col_ids == row_ids + d * slab, 1.0, 0.0).astype(BF16)
+    own_cols = dot(picker, whole, NT).astype(BF16)
+    rgram[m] = dot(own_cols, whole, NN).astype(BF16)
+    share(1, rgram)
+    for j in (1, 2, 3):
+        routes[1, j].wait_recv()
+    precond = dot(larr[owner_ref[m]], whole, NN).astype(BF16)
+    across = flip(m, 2)
+    for k, ref in ((0, lgram), (1, rgram)):
+        gram_copies[k, 0].wait_recv()
+        gram_copies[k, 2] = start(
+            remote(ref.at[across], ref.at[across], gram_ss.at[k, 2], gram_rs.at[k, 2], {"mp": flip(m, 1)})
+        )
+    for j in range(4):
+        right_copies["x%d" % j].wait_recv()
+    update_ref[...] = dot(precond, right[...], NN).astype(BF16)
+
+    picks = []
+    for s in range(capacity):
+        index, used = jnp.int32(0), jnp.int32(0)
+        for c in range(blocks):
+            hit = jnp.logical_and(owners[c] == m, rank_of(c) == s)
+            index = index + jnp.where(hit, c, 0).astype(jnp.int32)
+            used = used + jnp.where(hit, 1, 0).astype(jnp.int32)
+        picks.append((jnp.minimum(index, blocks - 1), used))
+    for k, (ref, stat, new) in enumerate(((lgram, lstat, left_new_ref), (rgram, rstat, right_new_ref))):
+        stats[k].wait()
+        gram_copies[k, 1].wait_recv()
+        gram_copies[k, 2].wait_recv()
+        for s, (index, used) in enumerate(picks):
+            old = stat[s]
+            fresh = 0.8 * old + 0.2 * (ref[index].astype(F32) / order)
+            new[s] = jnp.where(used > 0, fresh, old)
+    for copy in pending:
+        copy.wait_send()
+
+
+def fused_local(acts, out_grads, block_owner, left_stat, right_stat, left_root, right_root):
+    capacity, slab, order = left_stat.shape
+    blocks = block_owner.shape[0]
+    tokens = acts.shape[0]
+    width = out_grads.shape[1]
+    dma, vmem = pltpu.SemaphoreType.DMA, pltpu.VMEM
+    any_spec = pl.BlockSpec(memory_space=pl.ANY)
+    vmem_spec = pl.BlockSpec(memory_space=pltpu.VMEM)
+    return pl.pallas_call(
+        fused_kernel,
+        out_shape=(
+            jax.ShapeDtypeStruct((slab, width), BF16),
+            jax.ShapeDtypeStruct(left_stat.shape, F32),
+            jax.ShapeDtypeStruct(right_stat.shape, F32),
+        ),
+        in_specs=[pl.BlockSpec(memory_space=pltpu.SMEM)] + [any_spec] * 6,
+        out_specs=(vmem_spec,) * 3,
+        scratch_shapes=[
+            vmem((tokens, order), BF16),
+            vmem((tokens, width), BF16),
+            vmem(left_stat.shape, F32),
+            vmem(right_stat.shape, F32),
+            vmem(left_root.shape, BF16),
+            vmem(right_root.shape, BF16),
+            vmem((order, width), F32),
+        ]
+        + [vmem((4, slab, width), BF16)] * 4
+        + [vmem((order, width), BF16)] * 2
+        + [vmem((blocks, slab, order), BF16)] * 6
+        + [dma((4,)), dma((CHUNKS, 2))]
+        + [dma((2, 4))] * 2
+        + [dma((4,))] * 4
+        + [dma((2, 4))] * 4
+        + [dma((2, 3))] * 2,
+        compiler_params=pltpu.CompilerParams(
+            collective_id=0, has_side_effects=True, vmem_limit_bytes=48 * 1024 * 1024
+        ),
+        cost_estimate=pl.CostEstimate(
+            flops=2 * tokens * order * width, bytes_accessed=4 * tokens * order, transcendentals=0
+        ),
+    )(block_owner, acts, out_grads, left_stat, right_stat, left_root, right_root)
+
+
 def solution(mesh):
     in_specs = (
         P("dp", None),
@@ -111,4 +390,5 @@
         P("mp", "dp", None),
     )
     out_specs = (P("dp", "mp"), P("mp", "dp", None), P("mp", "dp", None))
+    local = fused_local if fits_fused(mesh.shape) else collective_local
     return jax.shard_map(local, mesh=mesh, in_specs=in_specs, out_specs=out_specs, check_vma=False)

time: 189 us -> 84.4 us (0.45); the launches traced: 186 us -> 84.1 us
  waiting for transfers between devices: 110 us -> 0 us
  Pallas kernels: 0 us -> 76.4 us
  matrix products: 18.9 us -> 0 us
  starting transfers between devices: 15.5 us -> 0 us
  blocking collectives: 15.1 us -> 0 us
  between operations: 15.7 us -> 0.65 us
  other arithmetic: 3.9 us -> 0 us
    pallas_call x0 -> x1, Pallas kernels: none -> 76.4 us  [fused_local(): pl.pallas_call(fused_kernel, out_shape=(jax.ShapeDtypeStruct((slab, width...]
    reduce_scatter x1 -> x0, waiting for transfers between devices: 70.1 us -> none  [local(): lax.psum_scatter(jnp.einsum('tr,tc->rc', acts, out_grads, preferred_eleme...]
    all_gather x2 -> x0, waiting for transfers between devices: 33.2 us -> none  [the longest x1 19.3 us: local(): lax.all_gather(right_rows, 'dp', axis=1, tiled=True)]
    dot_general x8 -> x0, matrix products: 18.9 us -> none  [the longest x1 5.98 us: local(): jnp.einsum('tr,tc->rc', acts, out_grads, preferred_element_type=jnp.float32)]
    all_to_all x3 -> x0, starting transfers between devices: 15.4 us -> none  [the longest x1 5.75 us: local(): lax.all_to_all(right_out, 'mp', split_axis=0, concat_axis=0, tiled=True)]
    all_to_all x1 -> x0, blocking collectives: 15.1 us -> none  [local(): lax.all_to_all(left_send.astype(jnp.bfloat16), 'mp', split_axis=0, concat...]
    all_to_all x3 -> x0, waiting for transfers between devices: 6.33 us -> none  [the longest x1 6.33 us: local(): lax.all_to_all(right_out, 'mp', split_axis=0, concat_axis=0, tiled=True)]
    unnamed x10 -> x13, local copies, waits for them, and re-layouts: 3.56 us -> 6.99 us
  transfers between devices with their start and end apart: 6 -> 0, of which waited for: 4 -> 0; matrix products, arithmetic and copies ran while one was open for 9% -> 0% of each run, Pallas kernels for 0% -> 0%
where the time goes in v1:
time: 84.4 us; the launch traced here: 84.1 us
  Pallas kernels  76.4 us (91%)
  local copies, waits for them, and re-layouts  6.99 us (8%)
    pallas_call x1, Pallas kernels, fused_local(): pl.pallas_call(fused_kernel, out_shape=(jax.ShapeDtypeStruct((slab, width...  76.4 us
    unnamed x13, local copies, waits for them, and re-layouts  6.99 us

profile of v1, /device:TPU:1, one launch (start us, length us, event | category | flops | bytes accessed | tf_op | source)
XLA Modules:
  0.0 84.1 jit_solution(5683137503355351580)
XLA Ops:
  0.6 0.0 copy-start
  0.6 1.1 %copy-done = f32[2,96,768]{2,1,0:T(8,128)S(1)} copy-done((f32[2,96,768]{2,1,0:T(8,128)S(1)}, f32[2,96,768]{2,1,0:T(8,128)}, u32[]{:S(2)}) %copy-start) | copy-done | bytes 589848
  1.7 0.0 copy-start.1
  1.7 1.1 %copy-done.1 = f32[2,96,768]{2,1,0:T(8,128)S(1)} copy-done((f32[2,96,768]{2,1,0:T(8,128)S(1)}, f32[2,96,768]{2,1,0:T(8,128)}, u32[]{:S(2)}) %copy-start.1) | copy-done | bytes 589848
  2.8 0.0 copy-start.2
  2.8 1.0 %copy-done.2 = bf16[2,96,768]{2,1,0:T(8,128)(2,1)S(1)} copy-done((bf16[2,96,768]{2,1,0:T(8,128)(2,1)S(1)}, bf16[2,96,768]{2,1,0:T(8,128)(2,1)}, u32[]{:S(2)}) %copy-start.2) | copy-done | bytes 294936
  3.7 0.0 copy-start.3
  3.7 1.0 %copy-done.3 = bf16[2,96,768]{2,1,0:T(8,128)(2,1)S(1)} copy-done((bf16[2,96,768]{2,1,0:T(8,128)(2,1)S(1)}, bf16[2,96,768]{2,1,0:T(8,128)(2,1)}, u32[]{:S(2)}) %copy-start.3) | copy-done | bytes 294936
  4.7 0.0 copy-start.4
  4.7 0.7 copy-done.4
  5.3 76.4 %shard_map.94 = (bf16[96,768]{1,0:T(8,128)(2,1)S(1)}, f32[2,96,768]{2,1,0:T(8,128)S(1)}, f32[2,96,768]{2,1,0:T(8,128)S(1)}) custom-call(s32[4]{0:T(128)S(1)} %copy-done.4, bf16[2048,768]{1,0:T(8,128)(2,1)} %acts_hbm.1, bf16[2048,768]{1,0:T(8,128)(2,1)} %outg_hbm.1, f32[2,96,768]{2,1,0:T(8,128)S(1)} %copy-done, f32[2,96,768]{2,1,0:T(8,128)S(1)} %copy-done.1, ...), custom_call_target="tpu_custom_call" | custom-call | flops 2415919104 | bytes 6291456 | tf_op jit(solution)/shard_map/pallas_call | solution.py:347
  81.8 0.7 copy.13
  82.4 0.8 copy.14
  83.3 0.8 copy.15
Async XLA Ops:
  0.6 1.1 %copy-start = (f32[2,96,768]{2,1,0:T(8,128)S(1)}, f32[2,96,768]{2,1,0:T(8,128)}, u32[]{:S(2)}) copy-start(f32[2,96,768]{2,1,0:T(8,128)} %left_stat_hbm.1) | copy-start | bytes 1769476
  1.7 1.1 %copy-start.1 = (f32[2,96,768]{2,1,0:T(8,128)S(1)}, f32[2,96,768]{2,1,0:T(8,128)}, u32[]{:S(2)}) copy-start(f32[2,96,768]{2,1,0:T(8,128)} %right_stat_hbm.1) | copy-start | bytes 1769476
  2.8 1.0 %copy-start.2 = (bf16[2,96,768]{2,1,0:T(8,128)(2,1)S(1)}, bf16[2,96,768]{2,1,0:T(8,128)(2,1)}, u32[]{:S(2)}) copy-start(bf16[2,96,768]{2,1,0:T(8,128)(2,1)} %left_root_hbm.1) | copy-start | bytes 884740
  3.7 1.0 %copy-start.3 = (bf16[2,96,768]{2,1,0:T(8,128)(2,1)S(1)}, bf16[2,96,768]{2,1,0:T(8,128)(2,1)}, u32[]{:S(2)}) copy-start(bf16[2,96,768]{2,1,0:T(8,128)(2,1)} %right_root_hbm.1) | copy-start | bytes 884740
  4.7 0.7 copy-start.4

commit v2 on v1

--- a/solution.py
+++ b/solution.py
@@ -136,9 +136,9 @@
     update_ref, left_new_ref, right_new_ref,
     acts, outg, lstat, rstat, lroot, rroot,
     part, send_x, recv_x, send_z, recv_z, grad, right,
-    lout, rout, larr, rarr, lgram, rgram,
+    lout, rout, larr, rarr, lgram, rgram, gram_out, update_out,
     load_sem, tok_sem, route_ss, route_rs, rsx_ss, rsx_rs, rsz_ss, rsz_rs,
-    agz_ss, agz_rs, agx_ss, agx_rs, gram_ss, gram_rs,
+    agz_ss, agz_rs, agc_ss, agc_rs, gram_ss, gram_rs, fwd_ss, upd_ss, upd_rs,
 ):
     blocks = owner_ref.shape[0]
     order = part.shape[0]
@@ -147,16 +147,19 @@
     chunk = acts.shape[0] // CHUNKS
     d, m = lax.axis_index("dp"), lax.axis_index("mp")
     z, x = d // 2, lax.rem(d, 2)
-
-    def dp_id(zz, xx):
-        return {"dp": zz * 2 + xx}
-
-    def rows_of(zz, xx):
-        return pl.ds(pl.multiple_of((zz * 2 + xx) * slab, slab), slab)
-
-    def remote(src, dst, ss, rs, device):
+    y, k = m // 2, lax.rem(m, 2)
+    turned = lax.rem(x + k, 2)
+    work = y * 2 + x
+
+    def device(zz, xx, yy, kk):
+        return {"dp": zz * 2 + xx, "mp": yy * 2 + kk}
+
+    def rows_of(zz, kk):
+        return pl.ds(pl.multiple_of((zz * 2 + kk) * slab, slab), slab)
+
+    def remote(src, dst, ss, rs, to):
         return pltpu.make_async_remote_copy(
-            src_ref=src, dst_ref=dst, send_sem=ss, recv_sem=rs, device_id=device, device_id_type=MESH
+            src_ref=src, dst_ref=dst, send_sem=ss, recv_sem=rs, device_id=to, device_id_type=MESH
         )
 
     loads = [
@@ -183,10 +186,13 @@
         copy.start()
 
     barrier = pltpu.get_barrier_semaphore()
-    partners = [dp_id(z, 1 - x)] + [dp_id(flip(z, j), x) for j in (1, 2, 3)]
-    partners += [{"mp": flip(m, j)} for j in (1, 2, 3)]
-    for device in partners:
-        pl.semaphore_signal(barrier, inc=1, device_id=device, device_id_type=MESH)
+    partners = [{"dp": flip(z, j) * 2 + x, "mp": m} for j in (1, 2, 3)]
+    partners += [
+        {"dp": z * 2 + xx, "mp": flip(m, j)}
+        for xx, j in [(x, 1), (x, 2), (x, 3)] + [(1 - x, j) for j in range(4)]
+    ]
+    for to in partners:
+        pl.semaphore_signal(barrier, inc=1, device_id=to, device_id_type=MESH)
 
     owners = [owner_ref[c] for c in range(blocks)]
 
@@ -201,26 +207,53 @@
     loads[0].wait()
     loads[1].wait()
     pl.semaphore_wait(barrier, len(partners))
-    pending = []
+    pending, pending_turned = [], []
 
     def start(copy):
         copy.start()
         pending.append(copy)
         return copy
 
-    routes = {}
-    for k, (root, out, arr) in enumerate(((rroot, rout, rarr), (lroot, lout, larr))):
-        for j in (2, 3, 1):
-            c = flip(m, j)
-            out[j] = root[rank_of(c)]
-            routes[k, j] = start(
-                remote(out.at[j], arr.at[m], route_ss.at[k, j], route_rs.at[k, j], {"mp": c})
-            )
-        arr[m] = root[rank_of(m)]
+    def route_copy(q, out, arr, j, source):
+        c = flip(work, j)
+        to = {"dp": z * 2 + lax.rem(c, 2), "mp": (c // 2) * 2 + x}
+        return remote(out.at[j], arr.at[source], route_ss.at[q, j], route_rs.at[q, source], to)
+
+    def route(q, root, out, arr):
+        for j in (3, 1, 2):
+            out[j] = root[rank_of(flip(work, j))]
+            start(route_copy(q, out, arr, j, m))
+        own = root[rank_of(work)]
+        out[0] = own
+        copy = route_copy(q, out, arr, 0, m)
+        pending_turned.append(copy)
+
+        @pl.when(turned == 1)
+        def _():
+            copy.start()
+
+        @pl.when(turned == 0)
+        def _():
+            arr[m] = own
+
+    def route_wait(q, out, arr):
+        for source in range(blocks):
+
+            @pl.when(jnp.logical_or(turned == 1, m != source))
+            def _(source=source):
+                route_copy(q, out, arr, 1, source).wait_recv()
+
+    route(0, rroot, rout, rarr)
 
     part[...] = jnp.zeros_like(part)
-    partner = dp_id(z, 1 - x)
-    sum_x = {}
+    first_core = k * turned + (1 - k) * (1 - turned)
+
+    def sum_x_copy(slot, into, j):
+        to = device(z, k, y, first_core if slot == 0 else 1 - k)
+        return remote(
+            send_x.at[slot, j], recv_x.at[into, j], rsx_ss.at[slot, j], rsx_rs.at[into, j], to
+        )
+
     for step in range(2):
         which = 1 - z // 2 if step == 0 else z // 2
         base = pl.multiple_of(which * half, half)
@@ -236,85 +269,130 @@
 
         lax.fori_loop(0, CHUNKS, token_step, 0)
         for j in ((2, 3), (1, 0))[step]:
-            send_x[j] = part[rows_of(flip(z, j), 1 - x), :].astype(BF16)
-            sum_x[j] = start(
-                remote(send_x.at[j], recv_x.at[j], rsx_ss.at[j], rsx_rs.at[j], partner)
-            )
-
-    me = rows_of(z, x)
-
-    def gather_own(k, ref):
-        copies = {"x0": start(remote(ref.at[me], ref.at[me], agx_ss.at[k, 0], agx_rs.at[k, 0], partner))}
+            send_x[0, j] = part[rows_of(flip(z, j), first_core), :].astype(BF16)
+            start(sum_x_copy(0, turned, j))
+            second = sum_x_copy(1, 1, j)
+            pending_turned.append(second)
+
+            @pl.when(turned == 1)
+            def _(j=j, second=second):
+                send_x[1, j] = part[rows_of(flip(z, j), 1 - k), :].astype(BF16)
+                second.start()
+
+    me = rows_of(z, k)
+    beside = {"mp": flip(m, 1)}
+
+    def gather_own(q, ref):
+        copies = {
+            "c0": start(remote(ref.at[me], ref.at[me], agc_ss.at[q, 0], agc_rs.at[q, 0], beside))
+        }
         for j in (2, 3, 1):
             copies[j] = start(
-                remote(ref.at[me], ref.at[me], agz_ss.at[k, j], agz_rs.at[k, j], dp_id(flip(z, j), x))
+                remote(
+                    ref.at[me], ref.at[me], agz_ss.at[q, j], agz_rs.at[q, j],
+                    {"dp": flip(z, j) * 2 + x},
+                )
             )
         return copies
 
-    def gather_on(k, ref, copies):
+    def gather_on(q, ref, copies):
         for j in (1, 2, 3):
             copies[j].wait_recv()
-            rows = rows_of(flip(z, j), x)
-            copies["x%d" % j] = start(
-                remote(ref.at[rows], ref.at[rows], agx_ss.at[k, j], agx_rs.at[k, j], partner)
+            rows = rows_of(flip(z, j), k)
+            copies["c%d" % j] = start(
+                remote(ref.at[rows], ref.at[rows], agc_ss.at[q, j], agc_rs.at[q, j], beside)
             )
 
-    for j in (1, 2, 3):
-        routes[0, j].wait_recv()
-    right[me, :] = rarr[owner_ref[m]]
+    route_wait(0, rout, rarr)
+    right[me, :] = rarr[owner_ref[work]]
     right_copies = gather_own(1, right)
 
     sum_z = {}
-    for j in (2, 3, 1):
-        sum_x[j].wait_recv()
-        send_z[j] = (part[rows_of(flip(z, j), x), :] + recv_x[j].astype(F32)).astype(BF16)
-        sum_z[j] = start(
-            remote(send_z.at[j], recv_z.at[j], rsz_ss.at[j], rsz_rs.at[j], dp_id(flip(z, j), x))
-        )
-    gather_on(1, right, right_copies)
-    sum_x[0].wait_recv()
-    total = part[me, :] + recv_x[0].astype(F32)
+    for j in (2, 3, 1, 0):
+        rows = rows_of(flip(z, j), k)
+
+        @pl.when(turned == 1)
+        def _(j=j, rows=rows):
+            sum_x_copy(0, 0, j).wait_recv()
+            part[rows, :] = recv_x[0, j].astype(F32)
+
+        sum_x_copy(0, 1, j).wait_recv()
+        both = part[rows, :] + recv_x[1, j].astype(F32)
+        if j == 0:
+            total = both
+        else:
+            send_z[j] = both.astype(BF16)
+            sum_z[j] = start(
+                remote(
+                    send_z.at[j], recv_z.at[j], rsz_ss.at[j], rsz_rs.at[j],
+                    {"dp": flip(z, j) * 2 + x},
+                )
+            )
+    route(1, lroot, lout, larr)
     for j in (1, 2, 3):
         sum_z[j].wait_recv()
         total = total + recv_z[j].astype(F32)
     own_grad = total.astype(BF16)
     grad[me, :] = own_grad
     copies = gather_own(0, grad)
+    gather_on(1, right, right_copies)
     gather_on(0, grad, copies)
     for j in range(4):
-        copies["x%d" % j].wait_recv()
+        copies["c%d" % j].wait_recv()
 
     whole = grad[...]
-    gram_copies = {}
-
-    def share(k, ref):
-        gram_copies[k, 0] = start(
-            remote(ref.at[m], ref.at[m], gram_ss.at[k, 0], gram_rs.at[k, 0], {"mp": flip(m, 2)})
-        )
-        gram_copies[k, 1] = start(
-            remote(ref.at[m], ref.at[m], gram_ss.at[k, 1], gram_rs.at[k, 1], {"mp": flip(m, 1)})
-        )
-
-    lgram[m] = dot(own_grad, whole, NT).astype(BF16)
-    share(0, lgram)
+
+    def gram_copy(q, way, block):
+        ref = (lgram, rgram)[q]
+        to = device(z, k, y, first_core) if way == 0 else device(z, k, 1 - y, k)
+        return remote(gram_out.at[q], ref.at[block], gram_ss.at[q, way], gram_rs.at[q, block], to)
+
+    def share(q, value):
+        gram_out[q] = value
+        start(gram_copy(q, 1, work))
+        start(gram_copy(q, 0, work))
+
+        @pl.when(turned == 0)
+        def _():
+            (lgram, rgram)[q][work] = value
+
+    share(0, dot(own_grad, whole, NT).astype(BF16))
     row_ids = lax.broadcasted_iota(jnp.int32, (slab, order), 0)
     col_ids = lax.broadcasted_iota(jnp.int32, (slab, order), 1)
-    picker = jnp.where(col_ids == row_ids + d * slab, 1.0, 0.0).astype(BF16)
+    picker = jnp.where(col_ids == row_ids + (z * 2 + k) * slab, 1.0, 0.0).astype(BF16)
     own_cols = dot(picker, whole, NT).astype(BF16)
-    rgram[m] = dot(own_cols, whole, NN).astype(BF16)
-    share(1, rgram)
-    for j in (1, 2, 3):
-        routes[1, j].wait_recv()
-    precond = dot(larr[owner_ref[m]], whole, NN).astype(BF16)
-    across = flip(m, 2)
-    for k, ref in ((0, lgram), (1, rgram)):
-        gram_copies[k, 0].wait_recv()
-        gram_copies[k, 2] = start(
-            remote(ref.at[across], ref.at[across], gram_ss.at[k, 2], gram_rs.at[k, 2], {"mp": flip(m, 1)})
-        )
+    share(1, dot(own_cols, whole, NN).astype(BF16))
+    route_wait(1, lout, larr)
+    precond = dot(larr[owner_ref[work]], whole, NN).astype(BF16)
     for j in range(4):
-        right_copies["x%d" % j].wait_recv()
-    update_ref[...] = dot(precond, right[...], NN).astype(BF16)
+        right_copies["c%d" % j].wait_recv()
+    update = dot(precond, right[...], NN).astype(BF16)
+    update_out[...] = update
+    update_copy = remote(
+        update_out, update_ref, upd_ss.at[0], upd_rs.at[0], device(z, k, y, x)
+    )
+
+    @pl.when(turned == 1)
+    def _():
+        update_copy.start()
+
+    def forward_copy(q, j):
+        ref, block = (lgram, rgram)[q], flip(work, j)
+        return remote(ref.at[block], ref.at[block], fwd_ss.at[q, j], gram_rs.at[q, block], beside)
+
+    @pl.when(turned == 0)
+    def _():
+        update_ref[...] = update
+        for q in range(2):
+            for j in (1, 2, 3):
+                gram_copy(q, 0, flip(work, j)).wait_recv()
+                forward_copy(q, j).start()
+
+    @pl.when(turned == 1)
+    def _():
+        for q in range(2):
+            for j in range(4):
+                gram_copy(q, 0, flip(work, j)).wait_recv()
 
     picks = []
     for s in range(capacity):
@@ -324,10 +402,8 @@
             index = index + jnp.where(hit, c, 0).astype(jnp.int32)
             used = used + jnp.where(hit, 1, 0).astype(jnp.int32)
         picks.append((jnp.minimum(index, blocks - 1), used))
-    for k, (ref, stat, new) in enumerate(((lgram, lstat, left_new_ref), (rgram, rstat, right_new_ref))):
-        stats[k].wait()
-        gram_copies[k, 1].wait_recv()
-        gram_copies[k, 2].wait_recv()
+    for q, (ref, stat, new) in enumerate(((lgram, lstat, left_new_ref), (rgram, rstat, right_new_ref))):
+        stats[q].wait()
         for s, (index, used) in enumerate(picks):
             old = stat[s]
             fresh = 0.8 * old + 0.2 * (ref[index].astype(F32) / order)
@@ -335,6 +411,19 @@
     for copy in pending:
         copy.wait_send()
 
+    @pl.when(turned == 0)
+    def _():
+        for q in range(2):
+            for j in (1, 2, 3):
+                forward_copy(q, j).wait_send()
+
+    @pl.when(turned == 1)
+    def _():
+        for copy in pending_turned:
+            copy.wait_send()
+        update_copy.wait_send()
+        update_copy.wait_recv()
+
 
 def fused_local(acts, out_grads, block_owner, left_stat, right_stat, left_root, right_root):
     capacity, slab, order = left_stat.shape
@@ -342,7 +431,7 @@
     tokens = acts.shape[0]
     width = out_grads.shape[1]
     dma, vmem = pltpu.SemaphoreType.DMA, pltpu.VMEM
-    any_spec = pl.BlockSpec(memory_space=pl.ANY)
+    any_spec = pl.BlockSpec(memory_space=pltpu.HBM)
     vmem_spec = pl.BlockSpec(memory_space=pltpu.VMEM)
     return pl.pallas_call(
         fused_kernel,
@@ -362,16 +451,18 @@
             vmem(right_root.shape, BF16),
             vmem((order, width), F32),
         ]
-        + [vmem((4, slab, width), BF16)] * 4
+        + [vmem((2, 4, slab, width), BF16)] * 2
+        + [vmem((4, slab, width), BF16)] * 2
         + [vmem((order, width), BF16)] * 2
         + [vmem((blocks, slab, order), BF16)] * 6
+        + [vmem((2, slab, order), BF16), vmem((slab, width), BF16)]
         + [dma((4,)), dma((CHUNKS, 2))]
-        + [dma((2, 4))] * 2
-        + [dma((4,))] * 4
         + [dma((2, 4))] * 4
-        + [dma((2, 3))] * 2,
+        + [dma((4,))] * 2
+        + [dma((2, 4))] * 4
+        + [dma((2, 2)), dma((2, 4)), dma((2, 4)), dma((1,)), dma((1,))],
         compiler_params=pltpu.CompilerParams(
-            collective_id=0, has_side_effects=True, vmem_limit_bytes=48 * 1024 * 1024
+            collective_id=0, has_side_effects=True, vmem_limit_bytes=56 * 1024 * 1024
         ),
         cost_estimate=pl.CostEstimate(
             flops=2 * tokens * order * width, bytes_accessed=4 * tokens * order, transcendentals=0

time: 84.4 us -> 74.8 us (0.89)
  Pallas kernels: 76.4 us -> 68.5 us
  local copies, waits for them, and re-layouts: 6.99 us -> 5.41 us
    pallas_call x1, Pallas kernels: 76.4 us -> 68.5 us  [fused_local(): pl.pallas_call(fused_kernel, out_shape=(jax.ShapeDtypeStruct((slab, width...]
    unnamed x13 -> x3, local copies, waits for them, and re-layouts: 6.99 us -> 5.41 us
where the time goes in v2:
time: 74.8 us; the launch traced here: 74.5 us
  Pallas kernels  68.5 us (92%)
  local copies, waits for them, and re-layouts  5.41 us (7%)
    pallas_call x1, Pallas kernels, fused_local(): pl.pallas_call(fused_kernel, out_shape=(jax.ShapeDtypeStruct((slab, width...  68.5 us
    unnamed x3, local copies, waits for them, and re-layouts  5.41 us

profile of v2, /device:TPU:1, one launch (start us, length us, event | category | flops | bytes accessed | tf_op | source)
XLA Modules:
  0.0 74.5 jit_solution(10232577727711491849)
XLA Ops:
  0.6 68.5 %shard_map.94 = (bf16[96,768]{1,0:T(8,128)(2,1)}, f32[2,96,768]{2,1,0:T(8,128)}, f32[2,96,768]{2,1,0:T(8,128)}) custom-call(s32[4]{0:T(128)} %owner_ref.1, bf16[2048,768]{1,0:T(8,128)(2,1)} %acts_hbm.1, bf16[2048,768]{1,0:T(8,128)(2,1)} %outg_hbm.1, f32[2,96,768]{2,1,0:T(8,128)} %left_stat_hbm.1, f32[2,96,768]{2,1,0:T(8,128)} %right_stat_hbm.1, ...), custom_call_target="tpu_custom_call" | custom-call | flops 2415919104 | bytes 6291456 | tf_op jit(solution)/shard_map/pallas_call | solution.py:436
  69.1 1.6 %copy.13 = bf16[96,768]{1,0:T(8,128)(2,1)} copy(bf16[96,768]{1,0:T(8,128)(2,1)} %get-tuple-element.6) | data formatting | bytes 294912
  70.7 1.9 %copy.14 = f32[2,96,768]{2,1,0:T(8,128)} copy(f32[2,96,768]{2,1,0:T(8,128)} %get-tuple-element.7) | data formatting | bytes 1179648
  72.6 1.9 %copy.15 = f32[2,96,768]{2,1,0:T(8,128)} copy(f32[2,96,768]{2,1,0:T(8,128)} %get-tuple-element.8) | data formatting | bytes 1179648

commit v3 on v2

--- a/solution.py
+++ b/solution.py
@@ -305,7 +305,6 @@
 
     route_wait(0, rout, rarr)
     right[me, :] = rarr[owner_ref[work]]
-    right_copies = gather_own(1, right)
 
     sum_z = {}
     for j in (2, 3, 1, 0):
@@ -335,7 +334,7 @@
     own_grad = total.astype(BF16)
     grad[me, :] = own_grad
     copies = gather_own(0, grad)
-    gather_on(1, right, right_copies)
+    right_copies = gather_own(1, right)
     gather_on(0, grad, copies)
     for j in range(4):
         copies["c%d" % j].wait_recv()
@@ -362,8 +361,20 @@
     picker = jnp.where(col_ids == row_ids + (z * 2 + k) * slab, 1.0, 0.0).astype(BF16)
     own_cols = dot(picker, whole, NT).astype(BF16)
     share(1, dot(own_cols, whole, NN).astype(BF16))
+    gather_on(1, right, right_copies)
     route_wait(1, lout, larr)
     precond = dot(larr[owner_ref[work]], whole, NN).astype(BF16)
+    def forward_copy(q, j):
+        ref, block = (lgram, rgram)[q], flip(work, j)
+        return remote(ref.at[block], ref.at[block], fwd_ss.at[q, j], gram_rs.at[q, block], beside)
+
+    @pl.when(turned == 0)
+    def _():
+        for q in range(2):
+            for j in (1, 2, 3):
+                gram_copy(q, 0, flip(work, j)).wait_recv()
+                forward_copy(q, j).start()
+
     for j in range(4):
         right_copies["c%d" % j].wait_recv()
     update = dot(precond, right[...], NN).astype(BF16)
@@ -376,17 +387,9 @@
     def _():
         update_copy.start()
 
-    def forward_copy(q, j):
-        ref, block = (lgram, rgram)[q], flip(work, j)
-        return remote(ref.at[block], ref.at[block], fwd_ss.at[q, j], gram_rs.at[q, block], beside)
-
     @pl.when(turned == 0)
     def _():
         update_ref[...] = update
-        for q in range(2):
-            for j in (1, 2, 3):
-                gram_copy(q, 0, flip(work, j)).wait_recv()
-                forward_copy(q, j).start()
 
     @pl.when(turned == 1)
     def _():

time: 74.8 us -> 69.4 us (0.928)
  the two profiles are of different devices: /device:TPU:1 before, /device:TPU:9 now
where the time goes in v3:
time: 69.4 us; the launch traced here: 69.2 us
  Pallas kernels  63.1 us (91%)
  local copies, waits for them, and re-layouts  5.41 us (8%)
    pallas_call x1, Pallas kernels, fused_local(): pl.pallas_call(fused_kernel, out_shape=(jax.ShapeDtypeStruct((slab, width...  63.1 us
    unnamed x3, local copies, waits for them, and re-layouts  5.41 us

profile of v3, /device:TPU:9, one launch (start us, length us, event | category | flops | bytes accessed | tf_op | source)
XLA Modules:
  0.0 69.2 jit_solution(10656797870539774057)
XLA Ops:
  0.6 63.1 %shard_map.94 = (bf16[96,768]{1,0:T(8,128)(2,1)}, f32[2,96,768]{2,1,0:T(8,128)}, f32[2,96,768]{2,1,0:T(8,128)}) custom-call(s32[4]{0:T(128)} %owner_ref.1, bf16[2048,768]{1,0:T(8,128)(2,1)} %acts_hbm.1, bf16[2048,768]{1,0:T(8,128)(2,1)} %outg_hbm.1, f32[2,96,768]{2,1,0:T(8,128)} %left_stat_hbm.1, f32[2,96,768]{2,1,0:T(8,128)} %right_stat_hbm.1, ...), custom_call_target="tpu_custom_call" | custom-call | flops 2415919104 | bytes 6291456 | tf_op jit(solution)/shard_map/pallas_call | solution.py:439
  63.7 1.6 %copy.13 = bf16[96,768]{1,0:T(8,128)(2,1)} copy(bf16[96,768]{1,0:T(8,128)(2,1)} %get-tuple-element.6) | data formatting | bytes 294912
  65.3 1.9 %copy.14 = f32[2,96,768]{2,1,0:T(8,128)} copy(f32[2,96,768]{2,1,0:T(8,128)} %get-tuple-element.7) | data formatting | bytes 1179648
  67.2 1.9 %copy.15 = f32[2,96,768]{2,1,0:T(8,128)} copy(f32[2,96,768]{2,1,0:T(8,128)} %get-tuple-element.8) | data formatting | bytes 1179648

commit v4 on v3

--- a/solution.py
+++ b/solution.py
@@ -204,8 +204,6 @@
             rank = rank + jnp.where(hit, 1, 0).astype(jnp.int32)
         return jnp.minimum(rank, capacity - 1)
 
-    loads[0].wait()
-    loads[1].wait()
     pl.semaphore_wait(barrier, len(partners))
     pending, pending_turned = [], []
 
@@ -243,7 +241,6 @@
             def _(source=source):
                 route_copy(q, out, arr, 1, source).wait_recv()
 
-    route(0, rroot, rout, rarr)
 
     part[...] = jnp.zeros_like(part)
     first_core = k * turned + (1 - k) * (1 - turned)
@@ -303,8 +300,6 @@
                 remote(ref.at[rows], ref.at[rows], agc_ss.at[q, j], agc_rs.at[q, j], beside)
             )
 
-    route_wait(0, rout, rarr)
-    right[me, :] = rarr[owner_ref[work]]
 
     sum_z = {}
     for j in (2, 3, 1, 0):
@@ -327,6 +322,9 @@
                     {"dp": flip(z, j) * 2 + x},
                 )
             )
+    loads[0].wait()
+    loads[1].wait()
+    route(0, rroot, rout, rarr)
     route(1, lroot, lout, larr)
     for j in (1, 2, 3):
         sum_z[j].wait_recv()
@@ -334,6 +332,8 @@
     own_grad = total.astype(BF16)
     grad[me, :] = own_grad
     copies = gather_own(0, grad)
+    route_wait(0, rout, rarr)
+    right[me, :] = rarr[owner_ref[work]]
     right_copies = gather_own(1, right)
     gather_on(0, grad, copies)
     for j in range(4):

time: 69.4 us -> 66.5 us (0.958)
  Pallas kernels: 63.1 us -> 60.2 us
    pallas_call x1, Pallas kernels: 63.1 us -> 60.2 us  [fused_local(): pl.pallas_call(fused_kernel, out_shape=(jax.ShapeDtypeStruct((slab, width...]
where the time goes in v4:
time: 66.5 us; the launch traced here: 66.2 us
  Pallas kernels  60.2 us (91%)
  local copies, waits for them, and re-layouts  5.41 us (8%)
    pallas_call x1, Pallas kernels, fused_local(): pl.pallas_call(fused_kernel, out_shape=(jax.ShapeDtypeStruct((slab, width...  60.2 us
    unnamed x3, local copies, waits for them, and re-layouts  5.41 us

profile of v4, /device:TPU:9, one launch (start us, length us, event | category | flops | bytes accessed | tf_op | source)
XLA Modules:
  0.0 66.2 jit_solution(11024650151455215227)
XLA Ops:
  0.6 60.2 %shard_map.94 = (bf16[96,768]{1,0:T(8,128)(2,1)}, f32[2,96,768]{2,1,0:T(8,128)}, f32[2,96,768]{2,1,0:T(8,128)}) custom-call(s32[4]{0:T(128)} %owner_ref.1, bf16[2048,768]{1,0:T(8,128)(2,1)} %acts_hbm.1, bf16[2048,768]{1,0:T(8,128)(2,1)} %outg_hbm.1, f32[2,96,768]{2,1,0:T(8,128)} %left_stat_hbm.1, f32[2,96,768]{2,1,0:T(8,128)} %right_stat_hbm.1, ...), custom_call_target="tpu_custom_call" | custom-call | flops 2415919104 | bytes 6291456 | tf_op jit(solution)/shard_map/pallas_call | solution.py:439
  60.8 1.6 %copy.13 = bf16[96,768]{1,0:T(8,128)(2,1)} copy(bf16[96,768]{1,0:T(8,128)(2,1)} %get-tuple-element.6) | data formatting | bytes 294912
  62.4 1.9 %copy.14 = f32[2,96,768]{2,1,0:T(8,128)} copy(f32[2,96,768]{2,1,0:T(8,128)} %get-tuple-element.7) | data formatting | bytes 1179648
  64.3 1.9 %copy.15 = f32[2,96,768]{2,1,0:T(8,128)} copy(f32[2,96,768]{2,1,0:T(8,128)} %get-tuple-element.8) | data formatting | bytes 1179648
